TPU v7x, 32 devices: a whole 2x2x4 slice. The times are simulated.
32 devices in a mesh: lat: 16 (over z, y, core), tgt: 2 (over x).
Axes of the slice: x: 2, y: 2, z: 4, core: 2. Of those that a mesh axis runs over, the one named last changes fastest.
Arguments:
- inputs: bfloat16 [128, 2, 2304], P('lat', None, 'tgt'), may hold values from -6 to 6
- w_enc: bfloat16 [2304, 32768], P('tgt', 'lat'), may hold values from -0.125 to 0.125
- b_enc: float32 [32768], P('lat'), may hold values from -4 to 4
- masks: int32 [128, 32768], P(None, 'lat'), may hold values 0 or 1
- w_dec: bfloat16 [2, 32768, 2304], P('tgt', 'lat'), may hold values from -0.046875 to 0.046875
- errors: bfloat16 [2, 128, 2304], P('tgt', 'lat'), may hold values from -6 to 6
- target_of: int32 [2], replicated, may hold values from 0 to 1, each once
Outputs:
- grad_enc: float32 [2304, 32768], P('tgt', 'lat')
- grad_bias: float32 [32768], P('lat')
- grad_in: float32 [128, 2, 2304], P('lat', None, 'tgt')
Inputs may be any that keep to these rules, and one draw needn't show every extreme that they name: `target_of`: each target layer names exactly one slot.
All inputs are finite; a program needn't handle non-finite values. No bound on the sum of `masks` on one device may be relied on, other than what follows from the above.
Results may differ from a plain program's by a relative error of at most 0.0029.
Values may be sent and summed in bfloat16 or wider, within the bound.
A program may use at most 64 MiB of HBM per device.

v0:
```python
import jax
import jax.numpy as jnp
from jax import lax
from jax.sharding import PartitionSpec as P

F = 16384
S = 2


penalty = 1.0
sharpness = 1.0


def latent_grad(dact, sumsq, act, gates):
    norm = jnp.sqrt(sumsq)[None, :]
    tanh_val = jnp.tanh(sharpness * act * norm)
    return (gates * (dact + penalty * sharpness * norm * (1.0 - tanh_val * tanh_val))).astype(
        jnp.bfloat16
    )


def local(inputs, w_enc, b_enc, masks, w_dec, errors, target_of):
    block = w_enc.shape[1]
    source = lax.axis_index("lat") * block // F
    slot = lax.axis_index("tgt")
    slots = jnp.arange(target_of.shape[0], dtype=jnp.int32)
    layer = jnp.sum(jnp.where(slots == slot, target_of, 0))
    flag = (layer >= source).astype(jnp.float32)
    gathered = lax.all_gather(inputs, "lat", axis=0, tiled=True)
    own = lax.dynamic_index_in_dim(gathered, source, 1, keepdims=False)
    partial_pre = jnp.dot(own, w_enc, preferred_element_type=jnp.float32)
    gates = masks.astype(jnp.float32)
    weights = w_dec[0]
    squares = flag * jnp.einsum("cd,cd->c", weights, weights, preferred_element_type=jnp.float32)
    term = flag * lax.dot_general(
        lax.all_gather(errors, "lat", axis=1, tiled=True)[0],
        weights,
        (((1,), (1,)), ((), ())),
        preferred_element_type=jnp.float32,
    )
    pre = lax.psum(partial_pre, "tgt") + b_enc[None, :]
    act = gates * pre
    dact, sumsq = lax.psum((term, squares), "tgt")
    grad = latent_grad(dact, sumsq, act, gates)
    grad_bias = jnp.sum(grad.astype(jnp.float32), axis=0)
    grad_enc = lax.dot_general(
        own, grad, (((0,), (0,)), ((), ())), preferred_element_type=jnp.float32
    )
    picker = (jnp.arange(S, dtype=jnp.int32) == source).astype(jnp.float32)
    part = lax.dot_general(
        grad, w_enc, (((1,), (1,)), ((), ())), preferred_element_type=jnp.float32
    )
    grad_in = lax.psum_scatter(
        part[:, None, :] * picker[None, :, None], "lat", scatter_dimension=0, tiled=True
    )
    return (grad_enc, grad_bias, grad_in)


def solution(mesh):
    return jax.shard_map(
        local,
        mesh=mesh,
        in_specs=(
            P("lat", None, "tgt"),
            P("tgt", "lat"),
            P("lat"),
            P(None, "lat"),
            P("tgt", "lat", None),
            P("tgt", "lat", None),
            P(),
        ),
        out_specs=(P("tgt", "lat"), P("lat"), P("lat", None, "tgt")),
        check_vma=False,
    )
```

profile of v0, /device:TPU:0, one launch (start us, length us, event | category | flops | bytes accessed | tf_op | source)
XLA Modules:
  0.0 236.3 jit_solution(1267833925207224575)
XLA Ops:
  7.2 0.0 all-reduce.7.cloned.1.call-start
  7.2 1.3 fusion.13
  9.2 0.8 copy.11
  10.0 24.8 %all_gather.6 = bf16[128,2,1152]{2,0,1:T(8,128)(2,1)S(1)} all-gather(bf16[8,2,1152]{2,0,1:T(8,128)(2,1)S(1)} %copy.11), channel_id=1, replica_groups=mesh['lat'=16,'tgt'=2] {'lat'}, dimensions={0}, use_global_device_ids=true | all-gather | bytes 626688 | tf_op jit(solution)/shard_map/all_gather | solution.py:29
  34.8 0.0 slice-start
  34.8 19.4 %all_gather.7 = bf16[1,128,2304]{2,1,0:T(8,128)(2,1)S(1)} all-gather(bf16[1,8,2304]{2,1,0:T(8,128)(2,1)} %param.12), channel_id=1, replica_groups=mesh['lat'=16,'tgt'=2] {'lat'}, dimensions={1}, use_global_device_ids=true | all-gather | bytes 626688 | tf_op jit(solution)/shard_map/all_gather | solution.py:36
  54.2 0.0 slice-start.1
  54.2 7.9 %fusion.3 = f32[128,2048]{1,0:T(8,128)} fusion(bf16[1,2048,2304]{2,1,0:T(8,128)(2,1)} %param.11, bf16[1,128,2304]{2,1,0:T(8,128)(2,1)S(1)} %all_gather.7, f32[]{:T(128)S(6)} %convert_element_type.20), kind=kOutput, calls=%fused_computation.4 | convolution fusion | flops 1208221696 | bytes 11075588 | tf_op jit(solution)/shard_map/dot_general | solution.py:35
  62.1 0.0 slice-done
  62.1 0.0 slice-done.1
  62.1 1.8 fusion.9
  64.0 0.0 all-reduce.7.cloned.1.call-update
  64.0 0.0 copy-start
  64.0 0.0 copy-start.1
  64.0 0.0 all-reduce.5.cloned.1.call-start
  64.1 5.7 %fusion = f32[2048]{0:T(1024)S(1)} fusion(bf16[1,2048,2304]{2,1,0:T(8,128)(2,1)} %param.11), kind=kLoop, calls=%fused_computation.1 | loop fusion | flops 14153728 | bytes 9445376 | tf_op jit(solution)/shard_map/cd,cd->c/dot_general | solution.py:34
  69.8 5.2 %psum.22 = f32[2048]{0:T(1024)S(1)} all-reduce(f32[2048]{0:T(1024)S(1)} %broadcast_multiply_fusion.1), channel_id=1, replica_groups=mesh['lat'=16,'tgt'=2] {'tgt'}, use_global_device_ids=true, to_apply=%region_2.3 | all-reduce | flops 2048 | bytes 16384 | tf_op jit(solution)/shard_map/psum | solution.py:43
  74.9 50.9 %all-reduce.7.cloned.1.call-done = (f32[128,2048]{1,0:T(8,128)}, f32[128,2048]{1,0:T(8,128)}) async-done(((f32[128,2048]{1,0:T(8,128)}, f32[128,2048]{1,0:T(8,128)}), (f32[128,2048]{1,0:T(8,128)}, f32[128,2048]{1,0:T(8,128)})) %all-reduce.7.cloned.1.call-update) | async-done | bytes 2097168 | tf_op jit(solution)/shard_map/psum | solution.py:43
  125.8 0.0 copy-done
  125.8 0.0 copy-done.1
  125.8 2.5 %convert_reduce_fusion = (f32[2048]{0:T(1024)}, bf16[128,2048]{1,0:T(8,128)(2,1)S(1)}) fusion(f32[128,2048]{1,0:T(8,128)} %get-tuple-element.3, f32[128,2048]{1,0:T(8,128)} %get-tuple-element.4, f32[2048]{0:T(1024)S(1)} %copy-done.1, f32[2048]{0:T(1024)S(1)} %sqrt.3, s32[128,2048]{1,0:T(8,128)S(1)} %copy-done), kind=kLoop, calls=%fused_computation.5 | loop fusion | flops 3143680 | bytes 3694592 | tf_op jit(solution)/shard_map/reduce_sum | solution.py:45
  128.4 0.0 copy-start.2
  128.4 4.0 %fusion.16 = f32[128,1152]{1,0:T(8,128)S(1)} fusion(bf16[128,2048]{1,0:T(8,128)(2,1)S(1)} %get-tuple-element.6, bf16[1152,2048]{1,0:T(8,128)(2,1)} %param.8), kind=kOutput, calls=%fused_computation.22 | convolution fusion | flops 603979776 | bytes 5832704 | tf_op jit(solution)/shard_map/dot_general | solution.py:50
  132.4 1.5 broadcast_multiply_fusion
  133.9 0.0 all-reduce.5.cloned.1.call-update
  133.9 0.0 copy-done.2
  133.9 0.6 dynamic-slice
  135.2 5.2 %fusion.7 = f32[1152,2048]{1,0:T(8,128)} fusion(bf16[128,2048]{1,0:T(8,128)(2,1)S(1)} %get-tuple-element.6, bf16[128,2,1152]{2,0,1:T(8,128)(2,1)S(1)} %all_gather.6, s32[]{:T(128)S(6)} %select_n.14), kind=kOutput, calls=%fused_computation.9 | convolution fusion | flops 603979776 | bytes 10256388 | tf_op jit(solution)/shard_map/dot_general | solution.py:46
  140.3 87.6 %all-reduce.5.cloned.1.call-done = f32[128,2,1152]{2,1,0:T(2,128)} async-done(((f32[128,2,1152]{2,1,0:T(2,128)}), f32[128,2,1152]{2,1,0:T(2,128)}) %all-reduce.5.cloned.1.call-update) | async-done | bytes 1179664
  227.9 1.5 constant_dynamic-slice_fusion
  (4 shorter events, 0.0 us)
Async XLA Ops:
  7.2 118.7 %all-reduce.7.cloned.1.call-start = ((), (), s32[]{:S(2)}) async-start(), calls=%async_computation.1 | async-start | bytes 4194304 | tf_op jit(solution)/shard_map/psum | solution.py:43
  34.8 27.4 %slice-start = ((s8[4718592]{0:T(1024)(128)(4,1)}), s8[524288]{0:T(1024)(128)(4,1)S(1)}, s32[]{:S(2)}) async-start(s8[4718592]{0:T(1024)(128)(4,1)} %bitcast.19), calls=%async_computation.2 | async-start | bytes 1048576
  54.2 7.9 %slice-start.1 = ((s8[4718592]{0:T(1024)(128)(4,1)}), s8[4194304]{0:T(1024)(128)(4,1)S(1)}, s32[]{:S(2)}) async-start(s8[4718592]{0:T(1024)(128)(4,1)} %bitcast.19), calls=%async_computation.3 | async-start | bytes 8388608
  64.0 61.8 %copy-start = (s32[128,2048]{1,0:T(8,128)S(1)}, s32[128,2048]{1,0:T(8,128)}, u32[]{:S(2)}) copy-start(s32[128,2048]{1,0:T(8,128)} %param.10) | copy-start | bytes 3145732
  64.0 61.8 %copy-start.1 = (f32[2048]{0:T(1024)S(1)}, f32[2048]{0:T(1024)}, u32[]{:S(2)}) copy-start(f32[2048]{0:T(1024)} %param.9) | copy-start | bytes 24580
  64.0 163.9 %all-reduce.5.cloned.1.call-start = ((), (), s32[]{:S(2)}) async-start(), calls=%async_computation | async-start | bytes 2359296
  128.4 5.5 %copy-start.2 = (u32[32]{0:T(128)S(1)}, u32[32]{0:T(128)}, u32[]{:S(2)}) copy-start(u32[32]{0:T(128)} %constant.42) | copy-start | bytes 388
Sparse Core Ops, SparseCore 0:
  64.1 61.6 all-reduce.6
  134.0 93.8 all-reduce.4
where the time goes:
time: 237 us; the launch traced here: 236 us
  waiting for transfers between devices  139 us (59%)
  blocking collectives  49.4 us (21%)
  matrix products  18.9 us (8%)
  between operations  15.4 us (6%)
  other arithmetic  11 us (5%)
  local copies, waits for them, and re-layouts  2.92 us (1%)
    unnamed x3, waiting for transfers between devices  87.6 us
    psum x1, waiting for transfers between devices, local(): dact, sumsq = lax.psum((term, squares), 'tgt')  50.9 us
    all_gather x1, blocking collectives, local(): gathered = lax.all_gather(inputs, 'lat', axis=0, tiled=True)  24.8 us
    all_gather x1, blocking collectives, local(): lax.all_gather(errors, 'lat', axis=1, tiled=True)[0]  19.4 us
    dot_general x1, matrix products, local(): lax.dot_general(lax.all_gather(errors, 'lat', axis=1, tiled=True)[0], wei...  7.93 us
    dot_general x1, other arithmetic, local(): jnp.einsum('cd,cd->c', weights, weights, preferred_element_type=jnp.float32)  5.67 us
    dot_general x1, matrix products, local(): lax.dot_general(own, grad, (((0,), (0,)), ((), ())), preferred_element_ty...  5.17 us
    psum x1, blocking collectives, local(): dact, sumsq = lax.psum((term, squares), 'tgt')  5.16 us
  transfers between devices with their start and end apart: 2, of which 2 were waited for; matrix products, arithmetic and copies ran while one was open for 5% of the time, Pallas kernels for 0%

commit v1 on v0

--- a/solution.py
+++ b/solution.py
@@ -1,11 +1,18 @@
+import functools
+
 import jax
 import jax.numpy as jnp
 from jax import lax
+from jax.experimental import pallas as pl
+from jax.experimental.pallas import tpu as pltpu
 from jax.sharding import PartitionSpec as P
 
 F = 16384
 S = 2
-
+MESH = pl.DeviceIdType.MESH
+Z = 4
+NT = 4
+TILE = 256
 
 penalty = 1.0
 sharpness = 1.0
@@ -19,7 +26,7 @@
     )
 
 
-def local(inputs, w_enc, b_enc, masks, w_dec, errors, target_of):
+def local_any(inputs, w_enc, b_enc, masks, w_dec, errors, target_of):
     block = w_enc.shape[1]
     source = lax.axis_index("lat") * block // F
     slot = lax.axis_index("tgt")
@@ -56,9 +63,333 @@
     return (grad_enc, grad_bias, grad_in)
 
 
+def tile_grad(dact, sumsq, act, gates):
+    norm = jnp.sqrt(sumsq)
+    tanh_val = jnp.tanh(sharpness * act * norm)
+    return gates * (dact + penalty * sharpness * norm * (1.0 - tanh_val * tanh_val))
+
+
+def kernel(
+    x_ref, we_hbm, b_ref, mask_hbm, wd_hbm, e_hbm, target_ref,
+    g_out, own_out, bias_out, in_out,
+    we, wd, mask, xs, es, xg, et, pre_send, pre_got, dact_send, dact_got,
+    sq_send, sq_own, sq_got, pre_own, dact_own, g_own, g_got, acc_t,
+    rs, rc, sums, ry, u, rz,
+    load_sem, xz_s, xz_r, xy_s, xy_r, xc_s, xc_r, ez_s, ez_r, ey_s, ey_r, ec_s, ec_r,
+    pre_s, pre_r, dact_s, dact_r, sq_s, sq_r, g_s, g_r, rs_s, rs_r, out_sem,
+):
+    f32 = jnp.float32
+    me = lax.axis_index("lat")
+    t = lax.axis_index("tgt")
+    z, y, c = me // 4, (me // 2) % 2, me % 2
+    source = z // (Z // S)
+    half = NT * TILE
+    far = [(z + k) % Z for k in range(Z)]
+    near = [(z + Z - k) % Z for k in range(Z)]
+
+    def lat_of(zz, yy, cc):
+        return (zz * 2 + yy) * 2 + cc
+
+    x_peer = (me, 1 - t)
+    y_peer = (lat_of(z, 1 - y, c), t)
+    c_peer = (lat_of(z, y, 1 - c), t)
+    z_peer = [(lat_of(far[k], y, c), t) for k in range(Z)]
+
+    def start_of(h):
+        return (t if h == 0 else 1 - t) * half
+
+    def we_load(h, j):
+        at = pl.multiple_of(start_of(h) + j * TILE, TILE)
+        return pltpu.make_async_copy(
+            we_hbm.at[:, pl.ds(at, TILE)], we.at[h, j], load_sem.at[h * NT + j]
+        )
+
+    def wd_load(h):
+        at = pl.multiple_of(start_of(h), half)
+        return pltpu.make_async_copy(wd_hbm.at[0, pl.ds(at, half)], wd.at[h], load_sem.at[2 * NT + h])
+
+    def mask_load(j):
+        at = pl.multiple_of(start_of(0) + j * TILE, TILE)
+        return pltpu.make_async_copy(
+            mask_hbm.at[:, pl.ds(at, TILE)], mask.at[j], load_sem.at[2 * NT + 2 + j]
+        )
+
+    e_load = pltpu.make_async_copy(e_hbm.at[0], es.at[c, z * 2 + y], load_sem.at[3 * NT + 2])
+    x_load = pltpu.make_async_copy(x_ref.at[source], xs.at[c, z * 2 + y], load_sem.at[3 * NT + 3])
+    x_load.start()
+    e_load.start()
+    for h in (1, 0):
+        for j in range(NT):
+            we_load(h, j).start()
+    wd_load(1).start()
+    wd_load(0).start()
+    for j in range(NT):
+        mask_load(j).start()
+
+    barrier = pltpu.get_barrier_semaphore()
+    for peer in [x_peer, y_peer, c_peer] + z_peer[1:]:
+        pl.semaphore_signal(barrier, inc=1, device_id=peer, device_id_type=MESH)
+    pl.semaphore_wait(barrier, Z + 2)
+
+    def remote(src, dst, send, recv, peer):
+        return pltpu.make_async_remote_copy(
+            src_ref=src, dst_ref=dst, send_sem=send, recv_sem=recv, device_id=peer, device_id_type=MESH
+        )
+
+    here = z * 2 + y
+    xz = [
+        remote(x_ref.at[far[k] // (Z // S)], xs.at[c, here], xz_s.at[k], xz_r.at[k], z_peer[k])
+        for k in range(1, Z)
+    ]
+    ez = [remote(e_hbm.at[0], es.at[c, here], ez_s.at[k], ez_r.at[k], z_peer[k]) for k in range(1, Z)]
+    for copy in xz + ez:
+        copy.start()
+
+    def along_y(buf, s, r):
+        return [
+            remote(buf.at[c, near[k] * 2 + y], buf.at[c, near[k] * 2 + y], s.at[k], r.at[k], y_peer)
+            for k in range(Z)
+        ]
+
+    def along_c(buf, s, r):
+        return [
+            remote(
+                buf.at[c, pl.ds(near[k] * 2, 2)], buf.at[c, pl.ds(near[k] * 2, 2)], s.at[k], r.at[k], c_peer
+            )
+            for k in range(Z)
+        ]
+
+    xy, xc = along_y(xs, xy_s, xy_r), along_c(xs, xc_s, xc_r)
+    ey, ec = along_y(es, ey_s, ey_r), along_c(es, ec_s, ec_r)
+
+    def z_to_y(load, along_z, y_copies):
+        load.wait()
+        y_copies[0].start()
+        for k in range(1, Z):
+            along_z[k - 1].wait_recv()
+            y_copies[k].start()
+
+    def y_to_c(y_copies, c_copies):
+        for k in range(Z):
+            y_copies[k].wait_recv()
+            c_copies[k].start()
+
+    def squares(h, out):
+        @pl.loop(0, NT)
+        def _(j):
+            total = jnp.zeros((TILE, 128), f32)
+            for at in range(0, wd.shape[2], 128):
+                w = wd[h, pl.ds(pl.multiple_of(j * TILE, TILE), TILE), at : at + 128].astype(f32)
+                total = total + w * w
+            out[j] = flag * jnp.sum(total.T, axis=0, keepdims=True)
+
+    flag = jnp.where(target_ref[t] >= source, 1.0, 0.0).astype(f32)
+
+    z_to_y(x_load, xz, xy)
+    wd_load(1).wait()
+    y_to_c(xy, xc)
+    z_to_y(e_load, ez, ey)
+    for copy in xc:
+        copy.wait_recv()
+    for q in range(Z * 2):
+        pair = jnp.concatenate([xs[0, q].astype(f32), xs[1, q].astype(f32)], axis=0)
+        xg[q * 16 : q * 16 + 16] = pair.astype(jnp.bfloat16)
+
+    for j in range(NT):
+        we_load(1, j).wait()
+
+    def pre_copy(j):
+        return remote(pre_send.at[j], pre_got.at[j], pre_s.at[j], pre_r.at[j], x_peer)
+
+    @pl.loop(0, NT)
+    def _(j):
+        part = jnp.dot(xg[...], we[1, j], preferred_element_type=f32)
+        pre_send[j] = part.astype(jnp.bfloat16)
+        pre_copy(j).start()
+
+    y_to_c(ey, ec)
+    squares(1, sq_send)
+    sq_copy = remote(sq_send, sq_got, sq_s.at[0], sq_r.at[0], x_peer)
+    sq_copy.start()
+    for j in range(NT):
+        we_load(0, j).wait()
+
+    @pl.loop(0, NT)
+    def _(j):
+        pre_own[j] = jnp.dot(xg[...], we[0, j], preferred_element_type=f32)
+
+    for copy in ec:
+        copy.wait_recv()
+    for q in range(0, Z * 2):
+        pair = jnp.concatenate([es[0, q].astype(f32), es[1, q].astype(f32)], axis=0)
+        et[q * 16 : q * 16 + 16] = pair.astype(jnp.bfloat16)
+
+    def dact_tile(h, j):
+        w = wd[h, pl.ds(pl.multiple_of(j * TILE, TILE), TILE)]
+        return flag * lax.dot_general(
+            et[...], w, (((1,), (1,)), ((), ())), preferred_element_type=f32
+        )
+
+    def dact_copy(j):
+        return remote(dact_send.at[j], dact_got.at[j], dact_s.at[j], dact_r.at[j], x_peer)
+
+    @pl.loop(0, NT)
+    def _(j):
+        dact_send[j] = dact_tile(1, j).astype(jnp.bfloat16)
+        dact_copy(j).start()
+
+    wd_load(0).wait()
+
+    @pl.loop(0, NT)
+    def _(j):
+        dact_own[j] = dact_tile(0, j)
+
+    squares(0, sq_own)
+    sq_copy.wait_recv()
+    for j in range(NT):
+        mask_load(j).wait()
+
+    def g_copy(j):
+        return remote(g_own.at[j], g_got.at[j], g_s.at[j], g_r.at[j], x_peer)
+
+    def input_part(w, grad):
+        return jnp.dot(w, grad.T.astype(jnp.bfloat16), preferred_element_type=f32)
+
+    acc_t[...] = jnp.zeros_like(acc_t)
+
+    @pl.loop(0, NT)
+    def _(j):
+        pre_copy(j).wait_recv()
+        dact_copy(j).wait_recv()
+        at = pl.multiple_of(start_of(0) + j * TILE, TILE)
+        gates = mask[j].astype(f32)
+        pre = pre_own[j] + pre_got[j].astype(f32) + b_ref[:, pl.ds(at, TILE)]
+        dact = dact_own[j] + dact_got[j].astype(f32)
+        grad = tile_grad(dact, sq_own[j] + sq_got[j], gates * pre, gates).astype(jnp.bfloat16)
+        g_own[j] = grad
+        g_copy(j).start()
+        grad = grad.astype(f32)
+        bias_out[:, pl.ds(at, TILE)] = jnp.sum(grad, axis=0, keepdims=True)
+        acc_t[...] += input_part(we[0, j], grad)
+
+    def g_store(h, j):
+        at = pl.multiple_of(start_of(h) + j * TILE, TILE)
+        buf = g_own if h == 0 else g_got
+        return pltpu.make_async_copy(buf.at[j], g_out.at[:, pl.ds(at, TILE)], out_sem.at[h * NT + j])
+
+    own_store = pltpu.make_async_copy(xg, own_out, out_sem.at[2 * NT])
+    own_store.start()
+    for j in range(NT):
+        g_store(0, j).start()
+
+    @pl.loop(0, NT)
+    def _(j):
+        g_copy(j).wait_recv()
+        g_store(1, j).start()
+        at = pl.multiple_of(start_of(1) + j * TILE, TILE)
+        grad = g_got[j].astype(f32)
+        bias_out[:, pl.ds(at, TILE)] = jnp.sum(grad, axis=0, keepdims=True)
+        acc_t[...] += input_part(we[1, j], grad)
+
+    part = acc_t[...].T
+    for zz in range(Z):
+        for yy in range(2):
+            for cc in range(2):
+                b = lat_of(zz, yy, cc)
+                rs[cc, yy, zz] = part[b * 8 : b * 8 + 8]
+    to_c = remote(rs.at[1 - c], rc, rs_s.at[0], rs_r.at[0], c_peer)
+    to_c.start()
+    to_c.wait_recv()
+    sums[...] = rs[c] + rc[...]
+    to_y = remote(sums.at[1 - y], ry, rs_s.at[1], rs_r.at[1], y_peer)
+    to_y.start()
+    to_y.wait_recv()
+    u[...] = sums[y] + ry[...]
+    to_z = [
+        remote(u.at[far[k]], rz.at[k], rs_s.at[1 + k], rs_r.at[1 + k], z_peer[k]) for k in range(1, Z)
+    ]
+    for copy in to_z:
+        copy.start()
+    terms = [u[z]]
+    for k in range(1, Z):
+        to_z[k - 1].wait_recv()
+        terms.append(rz[k])
+    for layer in range(S):
+        total = jnp.zeros_like(terms[0])
+        for k in range(Z):
+            total = total + jnp.where(near[k] // (Z // S) == layer, terms[k], 0.0)
+        in_out[layer] = total
+
+    for copy in xz + ez + xy + xc + ey + ec + [sq_copy, to_c, to_y] + to_z:
+        copy.wait_send()
+    for j in range(NT):
+        pre_copy(j).wait_send()
+        dact_copy(j).wait_send()
+        g_copy(j).wait_send()
+        g_store(0, j).wait()
+        g_store(1, j).wait()
+    own_store.wait()
+
+
+def local_kernel(inputs, w_enc, b_enc, masks, w_dec, errors, target_of):
+    rows, _, width = inputs.shape
+    tokens, block = masks.shape
+    full = w_dec.shape[2]
+    f32, bf16 = jnp.float32, jnp.bfloat16
+    vmem = pltpu.VMEM
+    dma = pltpu.SemaphoreType.DMA
+    hbm, whole = pl.BlockSpec(memory_space=pl.ANY), pl.BlockSpec(memory_space=pltpu.VMEM)
+    tiles = (NT, tokens, TILE)
+    grad, own, bias, grad_in = pl.pallas_call(
+        kernel,
+        out_shape=(
+            jax.ShapeDtypeStruct((tokens, block), bf16),
+            jax.ShapeDtypeStruct((tokens, width), bf16),
+            jax.ShapeDtypeStruct((1, block), f32),
+            jax.ShapeDtypeStruct((S, rows, width), f32),
+        ),
+        in_specs=[hbm, hbm, whole, hbm, hbm, hbm, pl.BlockSpec(memory_space=pltpu.SMEM)],
+        out_specs=(hbm, hbm, whole, whole),
+        scratch_shapes=[
+            vmem((2, NT, width, TILE), bf16),
+            vmem((2, NT * TILE, full), bf16),
+            vmem(tiles, jnp.int32),
+            vmem((2, Z * 2, rows, width), bf16),
+            vmem((2, Z * 2, rows, full), bf16),
+            vmem((tokens, width), bf16),
+            vmem((tokens, full), bf16),
+            vmem(tiles, bf16), vmem(tiles, bf16), vmem(tiles, bf16), vmem(tiles, bf16),
+            vmem((NT, 1, TILE), f32), vmem((NT, 1, TILE), f32), vmem((NT, 1, TILE), f32),
+            vmem(tiles, f32), vmem(tiles, f32),
+            vmem(tiles, bf16), vmem(tiles, bf16),
+            vmem((width, tokens), f32),
+            vmem((2, 2, Z, rows, width), f32),
+            vmem((2, Z, rows, width), f32),
+            vmem((2, Z, rows, width), f32),
+            vmem((Z, rows, width), f32),
+            vmem((Z, rows, width), f32),
+            vmem((Z, rows, width), f32),
+            dma((3 * NT + 4,)),
+        ]
+        + [dma((Z,))] * 12
+        + [dma((NT,))] * 4
+        + [dma((1,))] * 2
+        + [dma((NT,))] * 2
+        + [dma((Z + 1,))] * 2
+        + [dma((2 * NT + 1,))],
+        compiler_params=pltpu.CompilerParams(
+            collective_id=0, has_side_effects=True, vmem_limit_bytes=48 * 1024 * 1024
+        ),
+    )(jnp.transpose(inputs, (1, 0, 2)), w_enc, b_enc[None, :], masks, w_dec, errors, target_of)
+    grad_enc = lax.dot_general(own, grad, (((0,), (0,)), ((), ())), preferred_element_type=f32)
+    return grad_enc, bias[0], jnp.transpose(grad_in, (1, 0, 2))
+
+
 def solution(mesh):
+    sizes = dict(mesh.shape)
+    fits = sizes["lat"] == 4 * Z and sizes["tgt"] == 2
     return jax.shard_map(
-        local,
+        local_kernel if fits else local_any,
         mesh=mesh,
         in_specs=(
             P("lat", None, "tgt"),

time: 237 us -> 56.6 us (0.24)
  waiting for transfers between devices: 139 us -> 0 us
  blocking collectives: 49.4 us -> 0 us
  Pallas kernels: 0 us -> 44.7 us
  between operations: 15.4 us -> 0.64 us
  matrix products: 18.9 us -> 5.15 us
  other arithmetic: 11 us -> 0 us
  local copies, waits for them, and re-layouts: 2.92 us -> 5.39 us
    unnamed x3 -> x0, waiting for transfers between devices: 87.6 us -> none
    psum x1 -> x0, waiting for transfers between devices: 50.9 us -> none  [local(): dact, sumsq = lax.psum((term, squares), 'tgt')]
    pallas_call x0 -> x1, Pallas kernels: none -> 44.7 us  [local_kernel(): pl.pallas_call(kernel, out_shape=(jax.ShapeDtypeStruct((tokens, block), b...]
    all_gather x2 -> x0, blocking collectives: 44.2 us -> none  [the longest x1 24.8 us: local(): gathered = lax.all_gather(inputs, 'lat', axis=0, tiled=True)]
    dot_general x4 -> x1, matrix products: 18.9 us -> 5.15 us  [local_kernel(): lax.dot_general(own, grad, (((0,), (0,)), ((), ())), preferred_element_ty...]
    dot_general x1 -> x0, other arithmetic: 5.67 us -> none  [local(): jnp.einsum('cd,cd->c', weights, weights, preferred_element_type=jnp.float32)]
    psum x1 -> x0, blocking collectives: 5.16 us -> none  [local(): dact, sumsq = lax.psum((term, squares), 'tgt')]
    reduce_sum x2 -> x0, other arithmetic: 3.84 us -> none  [the longest x1 2.55 us: local(): grad_bias = jnp.sum(grad.astype(jnp.float32), axis=0)]
  transfers between devices with their start and end apart: 2 -> 0, of which waited for: 2 -> 0; matrix products, arithmetic and copies ran while one was open for 5% -> 0% of each run, Pallas kernels for 0% -> 0%
where the time goes in v1:
time: 56.6 us; the launch traced here: 55.9 us
  Pallas kernels  44.7 us (79%)
  local copies, waits for them, and re-layouts  5.39 us (10%)
  matrix products  5.15 us (9%)
  between operations  0.64 us (1%)
    pallas_call x1, Pallas kernels, local_kernel(): pl.pallas_call(kernel, out_shape=(jax.ShapeDtypeStruct((tokens, block), b...  44.7 us
    unnamed x11, local copies, waits for them, and re-layouts  5.39 us
    dot_general x1, matrix products, local_kernel(): lax.dot_general(own, grad, (((0,), (0,)), ((), ())), preferred_element_ty...  5.15 us

profile of v1, /device:TPU:0, one launch (start us, length us, event | category | flops | bytes accessed | tf_op | source)
XLA Modules:
  0.0 55.9 jit_solution(9281895951264840868)
XLA Ops:
  0.6 0.8 %copy.13 = bf16[8,2,1152]{2,0,1:T(8,128)(2,1)S(1)} copy(bf16[8,2,1152]{2,1,0:T(2,128)(2,1)} %param.7) | data formatting | bytes 73728 | tf_op args[0]
  1.4 0.0 copy-start
  1.4 1.2 %copy-done = s32[128,2048]{1,0:T(8,128)S(1)} copy-done((s32[128,2048]{1,0:T(8,128)S(1)}, s32[128,2048]{1,0:T(8,128)}, u32[]{:S(2)}) %copy-start) | copy-done | bytes 1048600
  2.6 0.0 copy-start.1
  2.6 0.8 %copy-done.1 = bf16[1,8,2304]{2,1,0:T(8,128)(2,1)S(1)} copy-done((bf16[1,8,2304]{2,1,0:T(8,128)(2,1)S(1)}, bf16[1,8,2304]{2,1,0:T(8,128)(2,1)}, u32[]{:S(2)}) %copy-start.1) | copy-done | bytes 36888
  3.4 0.0 copy-start.2
  3.4 0.7 %copy-done.2 = f32[2048]{0:T(1024)S(1)} copy-done((f32[2048]{0:T(1024)S(1)}, f32[2048]{0:T(1024)}, u32[]{:S(2)}) %copy-start.2) | copy-done | bytes 8216
  4.1 0.0 copy-start.3
  4.1 0.7 %copy-done.3 = s32[2]{0:T(128)S(1)} copy-done((s32[2]{0:T(128)S(1)}, s32[2]{0:T(128)}, u32[]{:S(2)}) %copy-start.3) | copy-done | bytes 32
  4.8 44.7 %shard_map.94 = (bf16[128,2048]{1,0:T(8,128)(2,1)S(1)}, bf16[128,1152]{1,0:T(8,128)(2,1)S(1)}, f32[1,2048]{1,0:T(1,128)S(1)}, f32[2,8,1152]{2,1,0:T(8,128)S(1)}) custom-call(bf16[2,8,1152]{2,1,0:T(8,128)(2,1)S(1)} %bitcast.8, bf16[1152,2048]{1,0:T(8,128)(2,1)} %we_hbm.1, f32[1,2048]{1,0:T(1,128)S(1)} %bitcast.10, s32[128,2048]{1,0:T(8,128)S(1)} %copy-done, ...), custom_call_target="tpu_custom_call" | custom-call | tf_op jit(solution)/shard_map/pallas_call | solution.py:343
  49.5 0.7 %copy.11 = f32[8,2,1152]{2,1,0:T(2,128)} copy(f32[8,2,1152]{2,0,1:T(8,128)S(1)} %bitcast.9) | data formatting | bytes 147456
  50.2 5.1 %fusion = f32[1152,2048]{1,0:T(8,128)} fusion(bf16[128,1152]{1,0:T(8,128)(2,1)S(1)} %get-tuple-element.7, bf16[128,2048]{1,0:T(8,128)(2,1)S(1)} %get-tuple-element.8), kind=kOutput, calls=%fused_computation.1 | convolution fusion | flops 603979776 | bytes 10256384 | tf_op jit(solution)/shard_map/dot_general | solution.py:384
  55.3 0.6 %copy.15 = f32[2048]{0:T(1024)} copy(f32[2048]{0:T(1024)S(1)} %bitcast.11) | data formatting | bytes 16384
Async XLA Ops:
  1.4 1.2 %copy-start = (s32[128,2048]{1,0:T(8,128)S(1)}, s32[128,2048]{1,0:T(8,128)}, u32[]{:S(2)}) copy-start(s32[128,2048]{1,0:T(8,128)} %mask_hbm.1) | copy-start | bytes 3145732
  2.6 0.8 %copy-start.1 = (bf16[1,8,2304]{2,1,0:T(8,128)(2,1)S(1)}, bf16[1,8,2304]{2,1,0:T(8,128)(2,1)}, u32[]{:S(2)}) copy-start(bf16[1,8,2304]{2,1,0:T(8,128)(2,1)} %e_hbm.1) | copy-start | bytes 110596
  3.4 0.7 %copy-start.2 = (f32[2048]{0:T(1024)S(1)}, f32[2048]{0:T(1024)}, u32[]{:S(2)}) copy-start(f32[2048]{0:T(1024)} %param.9) | copy-start | bytes 24580
  4.1 0.7 %copy-start.3 = (s32[2]{0:T(128)S(1)}, s32[2]{0:T(128)}, u32[]{:S(2)}) copy-start(s32[2]{0:T(128)} %target_ref.1) | copy-start | bytes 28

commit v2 on v1

--- a/solution.py
+++ b/solution.py
@@ -63,6 +63,9 @@
     return (grad_enc, grad_bias, grad_in)
 
 
+CHUNKS = 3
+
+
 def tile_grad(dact, sumsq, act, gates):
     norm = jnp.sqrt(sumsq)
     tanh_val = jnp.tanh(sharpness * act * norm)
@@ -70,13 +73,13 @@
 
 
 def kernel(
-    x_ref, we_hbm, b_ref, mask_hbm, wd_hbm, e_hbm, target_ref,
-    g_out, own_out, bias_out, in_out,
-    we, wd, mask, xs, es, xg, et, pre_send, pre_got, dact_send, dact_got,
+    x_hbm, we_hbm, b_hbm, mask_hbm, wd_hbm, e_hbm, target_ref,
+    g_out, own_out, in_out,
+    we, wd, mask, b_ref, x_raw, x_in, xs, es, xg, own_t, eg, et, pre_send, pre_got, dact_send, dact_got,
     sq_send, sq_own, sq_got, pre_own, dact_own, g_own, g_got, acc_t,
     rs, rc, sums, ry, u, rz,
     load_sem, xz_s, xz_r, xy_s, xy_r, xc_s, xc_r, ez_s, ez_r, ey_s, ey_r, ec_s, ec_r,
-    pre_s, pre_r, dact_s, dact_r, sq_s, sq_r, g_s, g_r, rs_s, rs_r, out_sem,
+    pre_s, pre_r, dact_s, dact_r, sq_s, sq_r, g_s, g_r, rc_s, rc_r, ry_s, ry_r, rz_s, rz_r, out_sem,
 ):
     f32 = jnp.float32
     me = lax.axis_index("lat")
@@ -104,31 +107,40 @@
             we_hbm.at[:, pl.ds(at, TILE)], we.at[h, j], load_sem.at[h * NT + j]
         )
 
-    def wd_load(h):
-        at = pl.multiple_of(start_of(h), half)
-        return pltpu.make_async_copy(wd_hbm.at[0, pl.ds(at, half)], wd.at[h], load_sem.at[2 * NT + h])
+    def wd_load(h, j):
+        at = pl.multiple_of(start_of(h) + j * TILE, TILE)
+        return pltpu.make_async_copy(
+            wd_hbm.at[0, pl.ds(at, TILE)], wd.at[h, j], load_sem.at[(2 + h) * NT + j]
+        )
 
     def mask_load(j):
         at = pl.multiple_of(start_of(0) + j * TILE, TILE)
         return pltpu.make_async_copy(
-            mask_hbm.at[:, pl.ds(at, TILE)], mask.at[j], load_sem.at[2 * NT + 2 + j]
+            mask_hbm.at[:, pl.ds(at, TILE)], mask.at[j], load_sem.at[4 * NT + j]
         )
 
-    e_load = pltpu.make_async_copy(e_hbm.at[0], es.at[c, z * 2 + y], load_sem.at[3 * NT + 2])
-    x_load = pltpu.make_async_copy(x_ref.at[source], xs.at[c, z * 2 + y], load_sem.at[3 * NT + 3])
+    e_load = pltpu.make_async_copy(e_hbm.at[0], es.at[c, z * 2 + y], load_sem.at[5 * NT])
+    x_load = pltpu.make_async_copy(x_hbm, x_raw, load_sem.at[5 * NT + 1])
+    b_load = pltpu.make_async_copy(b_hbm, b_ref, load_sem.at[5 * NT + 2])
     x_load.start()
     e_load.start()
     for h in (1, 0):
         for j in range(NT):
             we_load(h, j).start()
-    wd_load(1).start()
-    wd_load(0).start()
+        for j in range(NT):
+            wd_load(h, j).start()
+    b_load.start()
     for j in range(NT):
         mask_load(j).start()
 
     barrier = pltpu.get_barrier_semaphore()
     for peer in [x_peer, y_peer, c_peer] + z_peer[1:]:
         pl.semaphore_signal(barrier, inc=1, device_id=peer, device_id_type=MESH)
+    x_load.wait()
+    raw = x_raw[...].astype(f32)
+    for layer in range(S):
+        x_in[layer] = raw[:, layer, :].astype(jnp.bfloat16)
+    xs[c, z * 2 + y] = x_in[source]
     pl.semaphore_wait(barrier, Z + 2)
 
     def remote(src, dst, send, recv, peer):
@@ -138,7 +150,7 @@
 
     here = z * 2 + y
     xz = [
-        remote(x_ref.at[far[k] // (Z // S)], xs.at[c, here], xz_s.at[k], xz_r.at[k], z_peer[k])
+        remote(x_in.at[far[k] // (Z // S)], xs.at[c, here], xz_s.at[k], xz_r.at[k], z_peer[k])
         for k in range(1, Z)
     ]
     ez = [remote(e_hbm.at[0], es.at[c, here], ez_s.at[k], ez_r.at[k], z_peer[k]) for k in range(1, Z)]
@@ -162,8 +174,7 @@
     xy, xc = along_y(xs, xy_s, xy_r), along_c(xs, xc_s, xc_r)
     ey, ec = along_y(es, ey_s, ey_r), along_c(es, ec_s, ec_r)
 
-    def z_to_y(load, along_z, y_copies):
-        load.wait()
+    def z_to_y(along_z, y_copies):
         y_copies[0].start()
         for k in range(1, Z):
             along_z[k - 1].wait_recv()
@@ -174,21 +185,23 @@
             y_copies[k].wait_recv()
             c_copies[k].start()
 
-    def squares(h, out):
-        @pl.loop(0, NT)
-        def _(j):
-            total = jnp.zeros((TILE, 128), f32)
-            for at in range(0, wd.shape[2], 128):
-                w = wd[h, pl.ds(pl.multiple_of(j * TILE, TILE), TILE), at : at + 128].astype(f32)
-                total = total + w * w
-            out[j] = flag * jnp.sum(total.T, axis=0, keepdims=True)
+    def squares(h, j, out):
+        wd_load(h, j).wait()
+        total = jnp.zeros((TILE, 128), f32)
+        for at in range(0, wd.shape[3], 128):
+            w = wd[h, j, :, at : at + 128].astype(f32)
+            total = total + w * w
+        out[j] = flag * jnp.sum(total.T, axis=0, keepdims=True)
 
     flag = jnp.where(target_ref[t] >= source, 1.0, 0.0).astype(f32)
 
-    z_to_y(x_load, xz, xy)
-    wd_load(1).wait()
+    z_to_y(xz, xy)
+    squares(1, 0, sq_send)
     y_to_c(xy, xc)
-    z_to_y(e_load, ez, ey)
+    squares(1, 1, sq_send)
+    e_load.wait()
+    z_to_y(ez, ey)
+    pl.loop(2, NT)(lambda j: squares(1, j, sq_send))
     for copy in xc:
         copy.wait_recv()
     for q in range(Z * 2):
@@ -208,7 +221,6 @@
         pre_copy(j).start()
 
     y_to_c(ey, ec)
-    squares(1, sq_send)
     sq_copy = remote(sq_send, sq_got, sq_s.at[0], sq_r.at[0], x_peer)
     sq_copy.start()
     for j in range(NT):
@@ -218,17 +230,21 @@
     def _(j):
         pre_own[j] = jnp.dot(xg[...], we[0, j], preferred_element_type=f32)
 
+    pl.loop(0, NT)(lambda j: squares(0, j, sq_own))
+    for at in range(0, xg.shape[1], 128):
+        own_t[at : at + 128] = xg[:, at : at + 128].astype(f32).T.astype(jnp.bfloat16)
+    own_store = pltpu.make_async_copy(own_t, own_out, out_sem.at[2 * NT])
+    own_store.start()
     for copy in ec:
         copy.wait_recv()
     for q in range(0, Z * 2):
         pair = jnp.concatenate([es[0, q].astype(f32), es[1, q].astype(f32)], axis=0)
-        et[q * 16 : q * 16 + 16] = pair.astype(jnp.bfloat16)
+        eg[q * 16 : q * 16 + 16] = pair.astype(jnp.bfloat16)
+    for at in range(0, eg.shape[1], 128):
+        et[at : at + 128] = eg[:, at : at + 128].astype(f32).T.astype(jnp.bfloat16)
 
     def dact_tile(h, j):
-        w = wd[h, pl.ds(pl.multiple_of(j * TILE, TILE), TILE)]
-        return flag * lax.dot_general(
-            et[...], w, (((1,), (1,)), ((), ())), preferred_element_type=f32
-        )
+        return flag * jnp.dot(wd[h, j], et[...], preferred_element_type=f32).T
 
     def dact_copy(j):
         return remote(dact_send.at[j], dact_got.at[j], dact_s.at[j], dact_r.at[j], x_peer)
@@ -238,13 +254,11 @@
         dact_send[j] = dact_tile(1, j).astype(jnp.bfloat16)
         dact_copy(j).start()
 
-    wd_load(0).wait()
-
     @pl.loop(0, NT)
     def _(j):
         dact_own[j] = dact_tile(0, j)
 
-    squares(0, sq_own)
+    b_load.wait()
     sq_copy.wait_recv()
     for j in range(NT):
         mask_load(j).wait()
@@ -269,7 +283,6 @@
         g_own[j] = grad
         g_copy(j).start()
         grad = grad.astype(f32)
-        bias_out[:, pl.ds(at, TILE)] = jnp.sum(grad, axis=0, keepdims=True)
         acc_t[...] += input_part(we[0, j], grad)
 
     def g_store(h, j):
@@ -277,50 +290,60 @@
         buf = g_own if h == 0 else g_got
         return pltpu.make_async_copy(buf.at[j], g_out.at[:, pl.ds(at, TILE)], out_sem.at[h * NT + j])
 
-    own_store = pltpu.make_async_copy(xg, own_out, out_sem.at[2 * NT])
-    own_store.start()
     for j in range(NT):
         g_store(0, j).start()
 
-    @pl.loop(0, NT)
+    @pl.loop(0, NT - 1)
     def _(j):
         g_copy(j).wait_recv()
         g_store(1, j).start()
-        at = pl.multiple_of(start_of(1) + j * TILE, TILE)
-        grad = g_got[j].astype(f32)
-        bias_out[:, pl.ds(at, TILE)] = jnp.sum(grad, axis=0, keepdims=True)
-        acc_t[...] += input_part(we[1, j], grad)
-
-    part = acc_t[...].T
-    for zz in range(Z):
-        for yy in range(2):
-            for cc in range(2):
-                b = lat_of(zz, yy, cc)
-                rs[cc, yy, zz] = part[b * 8 : b * 8 + 8]
-    to_c = remote(rs.at[1 - c], rc, rs_s.at[0], rs_r.at[0], c_peer)
-    to_c.start()
-    to_c.wait_recv()
-    sums[...] = rs[c] + rc[...]
-    to_y = remote(sums.at[1 - y], ry, rs_s.at[1], rs_r.at[1], y_peer)
-    to_y.start()
-    to_y.wait_recv()
-    u[...] = sums[y] + ry[...]
+        acc_t[...] += input_part(we[1, j], g_got[j].astype(f32))
+
+    g_copy(NT - 1).wait_recv()
+    g_store(1, NT - 1).start()
+    last = g_got[NT - 1].astype(f32)
+    chunks = range(rs.shape[0])
+    wide = rs.shape[-1]
+    to_c = [remote(rs.at[d, 1 - c], rc.at[d], rc_s.at[d], rc_r.at[d], c_peer) for d in chunks]
+    to_y = [remote(sums.at[d, 1 - y], ry.at[d], ry_s.at[d], ry_r.at[d], y_peer) for d in chunks]
     to_z = [
-        remote(u.at[far[k]], rz.at[k], rs_s.at[1 + k], rs_r.at[1 + k], z_peer[k]) for k in range(1, Z)
+        remote(
+            u.at[d, far[k]], rz.at[d, k], rz_s.at[d * Z + k], rz_r.at[d * Z + k], z_peer[k]
+        )
+        for d in chunks
+        for k in range(1, Z)
     ]
-    for copy in to_z:
-        copy.start()
-    terms = [u[z]]
-    for k in range(1, Z):
-        to_z[k - 1].wait_recv()
-        terms.append(rz[k])
-    for layer in range(S):
-        total = jnp.zeros_like(terms[0])
-        for k in range(Z):
-            total = total + jnp.where(near[k] // (Z // S) == layer, terms[k], 0.0)
-        in_out[layer] = total
-
-    for copy in xz + ez + xy + xc + ey + ec + [sq_copy, to_c, to_y] + to_z:
+    for d in chunks:
+        at = d * wide
+        part = (acc_t[at : at + wide] + input_part(we[1, NT - 1, at : at + wide], last)).T
+        for zz in range(Z):
+            for yy in range(2):
+                for cc in range(2):
+                    b = lat_of(zz, yy, cc)
+                    rs[d, cc, yy, zz] = part[b * 8 : b * 8 + 8]
+        to_c[d].start()
+    for d in chunks:
+        to_c[d].wait_recv()
+        sums[d, 1 - y] = (rs[d, c, 1 - y] + rc[d, 1 - y]).astype(jnp.bfloat16)
+        to_y[d].start()
+        u[d] = rs[d, c, y] + rc[d, y]
+    for d in chunks:
+        to_y[d].wait_recv()
+        u[d] = u[d] + ry[d].astype(f32)
+        for copy in to_z[d * (Z - 1) : (d + 1) * (Z - 1)]:
+            copy.start()
+    for d in chunks:
+        terms = [u[d, z]]
+        for k in range(1, Z):
+            to_z[d * (Z - 1) + k - 1].wait_recv()
+            terms.append(rz[d, k])
+        for layer in range(S):
+            total = jnp.zeros_like(terms[0])
+            for k in range(Z):
+                total = total + jnp.where(near[k] // (Z // S) == layer, terms[k], 0.0)
+            in_out[layer, :, d * wide : (d + 1) * wide] = total
+
+    for copy in xz + ez + xy + xc + ey + ec + [sq_copy] + to_c + to_y + to_z:
         copy.wait_send()
     for j in range(NT):
         pre_copy(j).wait_send()
@@ -329,6 +352,16 @@
         g_store(0, j).wait()
         g_store(1, j).wait()
     own_store.wait()
+
+
+def encoder_kernel(own_ref, g_ref, in_ref, enc_out, bias_out, in_out):
+    @pl.when(pl.program_id(0) == 0)
+    def _():
+        bias_out[...] = jnp.sum(g_ref[...].astype(jnp.float32), axis=0, keepdims=True)
+        for layer in range(S):
+            in_out[:, layer, :] = in_ref[layer]
+
+    enc_out[...] = jnp.dot(own_ref[...], g_ref[...], preferred_element_type=jnp.float32)
 
 
 def local_kernel(inputs, w_enc, b_enc, masks, w_dec, errors, target_of):
@@ -338,51 +371,78 @@
     f32, bf16 = jnp.float32, jnp.bfloat16
     vmem = pltpu.VMEM
     dma = pltpu.SemaphoreType.DMA
-    hbm, whole = pl.BlockSpec(memory_space=pl.ANY), pl.BlockSpec(memory_space=pltpu.VMEM)
+    hbm = pl.BlockSpec(memory_space=pltpu.HBM)
+    free, whole = pl.BlockSpec(memory_space=pl.ANY), pl.BlockSpec(memory_space=pltpu.VMEM)
     tiles = (NT, tokens, TILE)
-    grad, own, bias, grad_in = pl.pallas_call(
+    wide = width // CHUNKS
+    grad, own_t, grad_in = pl.pallas_call(
         kernel,
         out_shape=(
             jax.ShapeDtypeStruct((tokens, block), bf16),
-            jax.ShapeDtypeStruct((tokens, width), bf16),
-            jax.ShapeDtypeStruct((1, block), f32),
+            jax.ShapeDtypeStruct((width, tokens), bf16),
             jax.ShapeDtypeStruct((S, rows, width), f32),
         ),
-        in_specs=[hbm, hbm, whole, hbm, hbm, hbm, pl.BlockSpec(memory_space=pltpu.SMEM)],
-        out_specs=(hbm, hbm, whole, whole),
+        in_specs=[hbm] * 6 + [pl.BlockSpec(memory_space=pltpu.SMEM)],
+        out_specs=(free, free, whole),
         scratch_shapes=[
             vmem((2, NT, width, TILE), bf16),
-            vmem((2, NT * TILE, full), bf16),
+            vmem((2, NT, TILE, full), bf16),
             vmem(tiles, jnp.int32),
+            vmem((1, block), f32),
+            vmem((rows, S, width), bf16),
+            vmem((S, rows, width), bf16),
             vmem((2, Z * 2, rows, width), bf16),
             vmem((2, Z * 2, rows, full), bf16),
             vmem((tokens, width), bf16),
+            vmem((width, tokens), bf16),
             vmem((tokens, full), bf16),
+            vmem((full, tokens), bf16),
             vmem(tiles, bf16), vmem(tiles, bf16), vmem(tiles, bf16), vmem(tiles, bf16),
             vmem((NT, 1, TILE), f32), vmem((NT, 1, TILE), f32), vmem((NT, 1, TILE), f32),
             vmem(tiles, f32), vmem(tiles, f32),
             vmem(tiles, bf16), vmem(tiles, bf16),
             vmem((width, tokens), f32),
-            vmem((2, 2, Z, rows, width), f32),
-            vmem((2, Z, rows, width), f32),
-            vmem((2, Z, rows, width), f32),
-            vmem((Z, rows, width), f32),
-            vmem((Z, rows, width), f32),
-            vmem((Z, rows, width), f32),
-            dma((3 * NT + 4,)),
+            vmem((CHUNKS, 2, 2, Z, rows, wide), f32),
+            vmem((CHUNKS, 2, Z, rows, wide), f32),
+            vmem((CHUNKS, 2, Z, rows, wide), bf16),
+            vmem((CHUNKS, Z, rows, wide), bf16),
+            vmem((CHUNKS, Z, rows, wide), f32),
+            vmem((CHUNKS, Z, rows, wide), f32),
+            dma((5 * NT + 3,)),
         ]
         + [dma((Z,))] * 12
         + [dma((NT,))] * 4
         + [dma((1,))] * 2
         + [dma((NT,))] * 2
-        + [dma((Z + 1,))] * 2
+        + [dma((CHUNKS,))] * 4
+        + [dma((CHUNKS * Z,))] * 2
         + [dma((2 * NT + 1,))],
         compiler_params=pltpu.CompilerParams(
-            collective_id=0, has_side_effects=True, vmem_limit_bytes=48 * 1024 * 1024
+            collective_id=0, has_side_effects=True, vmem_limit_bytes=62 * 1024 * 1024
         ),
-    )(jnp.transpose(inputs, (1, 0, 2)), w_enc, b_enc[None, :], masks, w_dec, errors, target_of)
-    grad_enc = lax.dot_general(own, grad, (((0,), (0,)), ((), ())), preferred_element_type=f32)
-    return grad_enc, bias[0], jnp.transpose(grad_in, (1, 0, 2))
+    )(inputs, w_enc, b_enc[None, :], masks, w_dec, errors, target_of)
+    step = width // 6
+    grad_enc, bias, grad_in = pl.pallas_call(
+        encoder_kernel,
+        grid=(width // step,),
+        out_shape=(
+            jax.ShapeDtypeStruct((width, block), f32),
+            jax.ShapeDtypeStruct((1, block), f32),
+            jax.ShapeDtypeStruct((rows, S, width), f32),
+        ),
+        in_specs=[
+            pl.BlockSpec((step, tokens), lambda i: (i, 0)),
+            pl.BlockSpec((tokens, block), lambda i: (0, 0)),
+            pl.BlockSpec((S, rows, width), lambda i: (0, 0, 0)),
+        ],
+        out_specs=(
+            pl.BlockSpec((step, block), lambda i: (i, 0)),
+            pl.BlockSpec((1, block), lambda i: (0, 0)),
+            pl.BlockSpec((rows, S, width), lambda i: (0, 0, 0)),
+        ),
+        compiler_params=pltpu.CompilerParams(vmem_limit_bytes=62 * 1024 * 1024),
+    )(own_t, grad, grad_in)
+    return grad_enc, bias[0], grad_in
 
 
 def solution(mesh):

time: 56.6 us -> 52.8 us (0.933)
  Pallas kernels: 44.7 us -> 51.8 us
  local copies, waits for them, and re-layouts: 5.39 us -> 0 us
  matrix products: 5.15 us -> 0 us
    pallas_call x0 -> x1, Pallas kernels: none -> 6.57 us  [local_kernel(): pl.pallas_call(encoder_kernel, grid=(width // step,), out_shape=(jax.Shap...]
    unnamed x11 -> x0, local copies, waits for them, and re-layouts: 5.39 us -> none
    dot_general x1 -> x0, matrix products: 5.15 us -> none  [local_kernel(): lax.dot_general(own, grad, (((0,), (0,)), ((), ())), preferred_element_ty...]
where the time goes in v2:
time: 52.8 us; the launch traced here: 52.5 us
  Pallas kernels  51.8 us (98%)
  between operations  0.64 us (1%)
    pallas_call x1, Pallas kernels, local_kernel(): pl.pallas_call(kernel, out_shape=(jax.ShapeDtypeStruct((tokens, block), b...  45.3 us
    pallas_call x1, Pallas kernels, local_kernel(): pl.pallas_call(encoder_kernel, grid=(width // step,), out_shape=(jax.Shap...  6.57 us

profile of v2, /device:TPU:0, one launch (start us, length us, event | category | flops | bytes accessed | tf_op | source)
XLA Modules:
  0.0 52.5 jit_solution(7934099623438738943)
XLA Ops:
  0.6 45.3 %shard_map.94 = (bf16[128,2048]{1,0:T(8,128)(2,1)}, bf16[1152,128]{1,0:T(8,128)(2,1)}, f32[2,8,1152]{2,1,0:T(8,128)}) custom-call(bf16[8,2,1152]{2,1,0:T(2,128)(2,1)} %x_hbm.1, bf16[1152,2048]{1,0:T(8,128)(2,1)} %we_hbm.1, f32[1,2048]{1,0:T(1,128)} %bitcast.2, s32[128,2048]{1,0:T(8,128)} %mask_hbm.1, bf16[1,2048,2304]{2,1,0:T(8,128)(2,1)} %wd_hbm.1, ...), custom_call_target="tpu_custom_call" | custom-call | tf_op jit(solution)/shard_map/pallas_call | solution.py:378
  45.9 6.6 %shard_map.95 = (f32[1152,2048]{1,0:T(8,128)}, f32[1,2048]{1,0:T(1,128)}, f32[8,2,1152]{2,1,0:T(2,128)}) custom-call(bf16[1152,128]{1,0:T(8,128)(2,1)} %get-tuple-element.9.own_ref, bf16[128,2048]{1,0:T(8,128)(2,1)} %get-tuple-element.10.g_ref, f32[2,8,1152]{2,1,0:T(8,128)} %get-tuple-element.11.in_ref), custom_call_target="tpu_custom_call" | custom-call | tf_op jit(solution)/shard_map/pallas_call | solution.py:425

commit v3 on v2

--- a/solution.py
+++ b/solution.py
@@ -124,14 +124,10 @@
     b_load = pltpu.make_async_copy(b_hbm, b_ref, load_sem.at[5 * NT + 2])
     x_load.start()
     e_load.start()
-    for h in (1, 0):
-        for j in range(NT):
-            we_load(h, j).start()
-        for j in range(NT):
-            wd_load(h, j).start()
-    b_load.start()
-    for j in range(NT):
-        mask_load(j).start()
+    for j in range(2):
+        wd_load(1, j).start()
+    for j in range(NT):
+        we_load(1, j).start()
 
     barrier = pltpu.get_barrier_semaphore()
     for peer in [x_peer, y_peer, c_peer] + z_peer[1:]:
@@ -156,6 +152,8 @@
     ez = [remote(e_hbm.at[0], es.at[c, here], ez_s.at[k], ez_r.at[k], z_peer[k]) for k in range(1, Z)]
     for copy in xz + ez:
         copy.start()
+    for j in range(2, NT):
+        wd_load(1, j).start()
 
     def along_y(buf, s, r):
         return [
@@ -198,9 +196,15 @@
     z_to_y(xz, xy)
     squares(1, 0, sq_send)
     y_to_c(xy, xc)
+    for j in range(NT):
+        we_load(0, j).start()
     squares(1, 1, sq_send)
     e_load.wait()
     z_to_y(ez, ey)
+    for j in range(NT):
+        wd_load(0, j).start()
+        mask_load(j).start()
+    b_load.start()
     pl.loop(2, NT)(lambda j: squares(1, j, sq_send))
     for copy in xc:
         copy.wait_recv()
@@ -355,9 +359,10 @@
 
 
 def encoder_kernel(own_ref, g_ref, in_ref, enc_out, bias_out, in_out):
+    bias_out[...] = jnp.sum(g_ref[...].astype(jnp.float32), axis=0, keepdims=True)
+
     @pl.when(pl.program_id(0) == 0)
     def _():
-        bias_out[...] = jnp.sum(g_ref[...].astype(jnp.float32), axis=0, keepdims=True)
         for layer in range(S):
             in_out[:, layer, :] = in_ref[layer]
 
@@ -421,23 +426,22 @@
             collective_id=0, has_side_effects=True, vmem_limit_bytes=62 * 1024 * 1024
         ),
     )(inputs, w_enc, b_enc[None, :], masks, w_dec, errors, target_of)
-    step = width // 6
     grad_enc, bias, grad_in = pl.pallas_call(
         encoder_kernel,
-        grid=(width // step,),
+        grid=(block // TILE,),
         out_shape=(
             jax.ShapeDtypeStruct((width, block), f32),
             jax.ShapeDtypeStruct((1, block), f32),
             jax.ShapeDtypeStruct((rows, S, width), f32),
         ),
         in_specs=[
-            pl.BlockSpec((step, tokens), lambda i: (i, 0)),
-            pl.BlockSpec((tokens, block), lambda i: (0, 0)),
+            pl.BlockSpec((width, tokens), lambda i: (0, 0)),
+            pl.BlockSpec((tokens, TILE), lambda i: (0, i)),
             pl.BlockSpec((S, rows, width), lambda i: (0, 0, 0)),
         ],
         out_specs=(
-            pl.BlockSpec((step, block), lambda i: (i, 0)),
-            pl.BlockSpec((1, block), lambda i: (0, 0)),
+            pl.BlockSpec((width, TILE), lambda i: (0, i)),
+            pl.BlockSpec((1, TILE), lambda i: (0, i)),
             pl.BlockSpec((rows, S, width), lambda i: (0, 0, 0)),
         ),
         compiler_params=pltpu.CompilerParams(vmem_limit_bytes=62 * 1024 * 1024),

time: 52.8 us -> 53.6 us (1.015)
  Pallas kernels: 51.8 us -> 52.6 us
    pallas_call x1, Pallas kernels: 6.57 us -> 7.34 us  [local_kernel(): pl.pallas_call(encoder_kernel, grid=(block // TILE,), out_shape=(jax.Shap...]
where the time goes in v3:
time: 53.6 us; the launch traced here: 53.2 us
  Pallas kernels  52.6 us (98%)
  between operations  0.64 us (1%)
    pallas_call x1, Pallas kernels, local_kernel(): pl.pallas_call(kernel, out_shape=(jax.ShapeDtypeStruct((tokens, block), b...  45.2 us
    pallas_call x1, Pallas kernels, local_kernel(): pl.pallas_call(encoder_kernel, grid=(block // TILE,), out_shape=(jax.Shap...  7.34 us

profile of v3, /device:TPU:0, one launch (start us, length us, event | category | flops | bytes accessed | tf_op | source)
XLA Modules:
  0.0 53.2 jit_solution(1509174929661974971)
XLA Ops:
  0.6 45.2 %shard_map.94 = (bf16[128,2048]{1,0:T(8,128)(2,1)}, bf16[1152,128]{1,0:T(8,128)(2,1)}, f32[2,8,1152]{2,1,0:T(8,128)}) custom-call(bf16[8,2,1152]{2,1,0:T(2,128)(2,1)} %x_hbm.1, bf16[1152,2048]{1,0:T(8,128)(2,1)} %we_hbm.1, f32[1,2048]{1,0:T(1,128)} %bitcast.2, s32[128,2048]{1,0:T(8,128)} %mask_hbm.1, bf16[1,2048,2304]{2,1,0:T(8,128)(2,1)} %wd_hbm.1, ...), custom_call_target="tpu_custom_call" | custom-call | tf_op jit(solution)/shard_map/pallas_call | solution.py:383
  45.9 7.3 %shard_map.95 = (f32[1152,2048]{1,0:T(8,128)}, f32[1,2048]{1,0:T(1,128)}, f32[8,2,1152]{2,1,0:T(2,128)}) custom-call(bf16[1152,128]{1,0:T(8,128)(2,1)} %get-tuple-element.9.own_ref, bf16[128,2048]{1,0:T(8,128)(2,1)} %get-tuple-element.10.g_ref, f32[2,8,1152]{2,1,0:T(8,128)} %get-tuple-element.11.in_ref), custom_call_target="tpu_custom_call" | custom-call | tf_op jit(solution)/shard_map/pallas_call | solution.py:429

commit v4 on v2

v4 whole, which is shorter than its diff:
```python
import functools

import jax
import jax.numpy as jnp
from jax import lax
from jax.experimental import pallas as pl
from jax.experimental.pallas import tpu as pltpu
from jax.sharding import PartitionSpec as P

F = 16384
S = 2
MESH = pl.DeviceIdType.MESH
Z = 4
NT = 8
TILE = 256

penalty = 1.0
sharpness = 1.0


def latent_grad(dact, sumsq, act, gates):
    norm = jnp.sqrt(sumsq)[None, :]
    tanh_val = jnp.tanh(sharpness * act * norm)
    return (gates * (dact + penalty * sharpness * norm * (1.0 - tanh_val * tanh_val))).astype(
        jnp.bfloat16
    )


def local_any(inputs, w_enc, b_enc, masks, w_dec, errors, target_of):
    block = w_enc.shape[1]
    source = lax.axis_index("lat") * block // F
    slot = lax.axis_index("tgt")
    slots = jnp.arange(target_of.shape[0], dtype=jnp.int32)
    layer = jnp.sum(jnp.where(slots == slot, target_of, 0))
    flag = (layer >= source).astype(jnp.float32)
    gathered = lax.all_gather(inputs, "lat", axis=0, tiled=True)
    own = lax.dynamic_index_in_dim(gathered, source, 1, keepdims=False)
    partial_pre = jnp.dot(own, w_enc, preferred_element_type=jnp.float32)
    gates = masks.astype(jnp.float32)
    weights = w_dec[0]
    squares = flag * jnp.einsum("cd,cd->c", weights, weights, preferred_element_type=jnp.float32)
    term = flag * lax.dot_general(
        lax.all_gather(errors, "lat", axis=1, tiled=True)[0],
        weights,
        (((1,), (1,)), ((), ())),
        preferred_element_type=jnp.float32,
    )
    pre = lax.psum(partial_pre, "tgt") + b_enc[None, :]
    act = gates * pre
    dact, sumsq = lax.psum((term, squares), "tgt")
    grad = latent_grad(dact, sumsq, act, gates)
    grad_bias = jnp.sum(grad.astype(jnp.float32), axis=0)
    grad_enc = lax.dot_general(
        own, grad, (((0,), (0,)), ((), ())), preferred_element_type=jnp.float32
    )
    picker = (jnp.arange(S, dtype=jnp.int32) == source).astype(jnp.float32)
    part = lax.dot_general(
        grad, w_enc, (((1,), (1,)), ((), ())), preferred_element_type=jnp.float32
    )
    grad_in = lax.psum_scatter(
        part[:, None, :] * picker[None, :, None], "lat", scatter_dimension=0, tiled=True
    )
    return (grad_enc, grad_bias, grad_in)


CHUNKS = 3


def tile_grad(dact, sumsq, act, gates):
    norm = jnp.sqrt(sumsq)
    tanh_val = jnp.tanh(sharpness * act * norm)
    return gates * (dact + penalty * sharpness * norm * (1.0 - tanh_val * tanh_val))


def kernel(
    x_hbm, we_hbm, b_hbm, mask_hbm, wd_hbm, e_hbm, target_ref,
    g_out, own_out, in_out,
    we, wd, mask, b_ref, x_raw, x_in, xs, es, xg, own_t, eg, et, pre_send, pre_got, dact_send, dact_got,
    sq_own, sq_got, pre_own, dact_own, g_own, g_got, acc_t,
    rs, rc, sums, ry, u, rz,
    load_sem, xz_s, xz_r, xy_s, xy_r, xc_s, xc_r, ez_s, ez_r, ey_s, ey_r, ec_s, ec_r,
    pre_s, pre_r, dact_s, dact_r, sq_s, sq_r, g_s, g_r, rc_s, rc_r, ry_s, ry_r, rz_s, rz_r, out_sem,
):
    f32 = jnp.float32
    half = mask.shape[1]
    me = lax.axis_index("lat")
    t = lax.axis_index("tgt")
    z, y, c = me // 4, (me // 2) % 2, me % 2
    source = z // (Z // S)
    far = [(z + k) % Z for k in range(Z)]
    near = [(z + Z - k) % Z for k in range(Z)]

    def lat_of(zz, yy, cc):
        return (zz * 2 + yy) * 2 + cc

    x_peer = (me, 1 - t)
    y_peer = (lat_of(z, 1 - y, c), t)
    c_peer = (lat_of(z, y, 1 - c), t)
    z_peer = [(lat_of(far[k], y, c), t) for k in range(Z)]

    def we_load(j):
        return pltpu.make_async_copy(
            we_hbm.at[:, pl.ds(pl.multiple_of(j * TILE, TILE), TILE)], we.at[j], load_sem.at[j]
        )

    def wd_load(j):
        return pltpu.make_async_copy(
            wd_hbm.at[0, pl.ds(pl.multiple_of(j * TILE, TILE), TILE)], wd.at[j], load_sem.at[NT + j]
        )

    def mask_load(j):
        return pltpu.make_async_copy(
            mask_hbm.at[pl.ds(t * half, half), pl.ds(pl.multiple_of(j * TILE, TILE), TILE)],
            mask.at[j],
            load_sem.at[2 * NT + j],
        )

    e_load = pltpu.make_async_copy(e_hbm.at[0], es.at[c, z * 2 + y], load_sem.at[3 * NT])
    x_load = pltpu.make_async_copy(x_hbm, x_raw, load_sem.at[3 * NT + 1])
    b_load = pltpu.make_async_copy(b_hbm, b_ref, load_sem.at[3 * NT + 2])
    x_load.start()
    e_load.start()
    for j in range(NT):
        we_load(j).start()

    barrier = pltpu.get_barrier_semaphore()
    for peer in [x_peer, y_peer, c_peer] + z_peer[1:]:
        pl.semaphore_signal(barrier, inc=1, device_id=peer, device_id_type=MESH)
    x_load.wait()
    raw = x_raw[...].astype(f32)
    for layer in range(S):
        x_in[layer] = raw[:, layer, :].astype(jnp.bfloat16)
    xs[c, z * 2 + y] = x_in[source]
    pl.semaphore_wait(barrier, Z + 2)

    def remote(src, dst, send, recv, peer):
        return pltpu.make_async_remote_copy(
            src_ref=src, dst_ref=dst, send_sem=send, recv_sem=recv, device_id=peer, device_id_type=MESH
        )

    here = z * 2 + y
    xz = [
        remote(x_in.at[far[k] // (Z // S)], xs.at[c, here], xz_s.at[k], xz_r.at[k], z_peer[k])
        for k in range(1, Z)
    ]
    ez = [remote(e_hbm.at[0], es.at[c, here], ez_s.at[k], ez_r.at[k], z_peer[k]) for k in range(1, Z)]
    for copy in xz:
        copy.start()
    for j in range(NT):
        wd_load(j).start()

    def along_y(buf, s, r):
        return [
            remote(buf.at[c, near[k] * 2 + y], buf.at[c, near[k] * 2 + y], s.at[k], r.at[k], y_peer)
            for k in range(Z)
        ]

    def along_c(buf, s, r):
        return [
            remote(
                buf.at[c, pl.ds(near[k] * 2, 2)], buf.at[c, pl.ds(near[k] * 2, 2)], s.at[k], r.at[k], c_peer
            )
            for k in range(Z)
        ]

    xy, xc = along_y(xs, xy_s, xy_r), along_c(xs, xc_s, xc_r)
    ey, ec = along_y(es, ey_s, ey_r), along_c(es, ec_s, ec_r)

    def z_to_y(along_z, y_copies):
        y_copies[0].start()
        for k in range(1, Z):
            along_z[k - 1].wait_recv()
            y_copies[k].start()

    def y_to_c(y_copies, c_copies):
        for k in range(Z):
            y_copies[k].wait_recv()
            c_copies[k].start()

    def squares(j):
        wd_load(j).wait()
        total = jnp.zeros((TILE, 128), f32)
        for at in range(0, wd.shape[2], 128):
            w = wd[j, :, at : at + 128].astype(f32)
            total = total + w * w
        sq_own[j] = flag * jnp.sum(total.T, axis=0, keepdims=True)

    flag = jnp.where(target_ref[t] >= source, 1.0, 0.0).astype(f32)

    z_to_y(xz, xy)
    for copy in ez:
        copy.start()
    squares(0)
    y_to_c(xy, xc)
    for j in range(NT):
        mask_load(j).start()
    b_load.start()
    squares(1)
    e_load.wait()
    z_to_y(ez, ey)
    pl.loop(2, 4)(squares)
    for copy in xc:
        copy.wait_recv()

    def tokens_of(buf, out):
        for q in range(Z * 2):
            at = (q + t * Z) % (Z * 2)
            pair = jnp.concatenate([buf[0, at].astype(f32), buf[1, at].astype(f32)], axis=0)
            out[q * 16 : q * 16 + 16] = pair.astype(jnp.bfloat16)

    tokens_of(xs, xg)

    def pre_copy(j):
        return remote(pre_send.at[j], pre_got.at[j], pre_s.at[j], pre_r.at[j], x_peer)

    def pre_tile(j):
        we_load(j).wait()
        part = jnp.dot(xg[...], we[j], preferred_element_type=f32)
        pre_own[j] = part[:half]
        pre_send[j] = part[half:].astype(jnp.bfloat16)
        pre_copy(j).start()

    pl.loop(0, NT)(pre_tile)
    y_to_c(ey, ec)
    pl.loop(4, NT)(squares)
    sq_copy = remote(sq_own, sq_got, sq_s.at[0], sq_r.at[0], x_peer)
    sq_copy.start()
    for at in range(0, xg.shape[1], 128):
        own_t[at : at + 128] = xg[:, at : at + 128].astype(f32).T.astype(jnp.bfloat16)
    own_store = pltpu.make_async_copy(own_t, own_out, out_sem.at[2 * NT])
    own_store.start()
    for copy in ec:
        copy.wait_recv()
    tokens_of(es, eg)
    for at in range(0, eg.shape[1], 128):
        et[at : at + 128] = eg[:, at : at + 128].astype(f32).T.astype(jnp.bfloat16)

    def dact_copy(j):
        return remote(dact_send.at[j], dact_got.at[j], dact_s.at[j], dact_r.at[j], x_peer)

    def dact_tile(j):
        part = flag * jnp.dot(wd[j], et[...], preferred_element_type=f32).T
        dact_own[j] = part[:half]
        dact_send[j] = part[half:].astype(jnp.bfloat16)
        dact_copy(j).start()

    pl.loop(0, NT)(dact_tile)
    b_load.wait()
    sq_copy.wait_recv()

    def g_copy(j):
        return remote(g_own.at[j], g_got.at[j], g_s.at[j], g_r.at[j], x_peer)

    def g_store(h, j):
        buf = g_own if h == 0 else g_got
        at = pl.ds(pl.multiple_of(j * TILE, TILE), TILE)
        return pltpu.make_async_copy(
            buf.at[j], g_out.at[h * half : h * half + half, at], out_sem.at[h * NT + j]
        )

    def input_part(w, grad):
        return jnp.dot(w, grad.T.astype(jnp.bfloat16), preferred_element_type=f32)

    acc_t[...] = jnp.zeros_like(acc_t)

    def grad_tile(j):
        mask_load(j).wait()
        pre_copy(j).wait_recv()
        dact_copy(j).wait_recv()
        gates = mask[j].astype(f32)
        bias = b_ref[:, pl.ds(pl.multiple_of(j * TILE, TILE), TILE)]
        pre = pre_own[j] + pre_got[j].astype(f32) + bias
        dact = dact_own[j] + dact_got[j].astype(f32)
        grad = tile_grad(dact, sq_own[j] + sq_got[j], gates * pre, gates).astype(jnp.bfloat16)
        g_own[j] = grad
        g_copy(j).start()
        g_store(0, j).start()
        acc_t[0] += input_part(we[j], grad.astype(f32))

    pl.loop(0, NT)(grad_tile)

    chunks = range(rs.shape[1])
    wide = rs.shape[-1]
    slots = [(h, d) for h in range(2) for d in chunks]

    def sum_copies(src, dst, s, r, other, peer):
        return {
            (h, d): remote(src.at[h, d, other], dst.at[h, d], s.at[h, d], r.at[h, d], peer)
            for h, d in slots
        }

    to_c = sum_copies(rs, rc, rc_s, rc_r, 1 - c, c_peer)
    to_y = sum_copies(sums, ry, ry_s, ry_r, 1 - y, y_peer)
    to_z = {
        (d, k): remote(u.at[d, far[k]], rz.at[d, k], rz_s.at[d, k], rz_r.at[d, k], z_peer[k])
        for d in chunks
        for k in range(1, Z)
    }

    def over_c(h, d, part):
        part = part.T
        for b in range(half // 8):
            rs[h, d, b % 2, (b // 2) % 2, b // 4] = part[b * 8 : b * 8 + 8]
        to_c[h, d].start()

    def over_y(h, d):
        to_c[h, d].wait_recv()
        sums[h, d, 1 - y] = (rs[h, d, c, 1 - y] + rc[h, d, 1 - y]).astype(jnp.bfloat16)
        to_y[h, d].start()

    def over_z(h, d):
        group = t if h == 0 else 1 - t
        to_y[h, d].wait_recv()
        total = rs[h, d, c, y] + rc[h, d, y] + ry[h, d].astype(f32)
        for zz in range(Z // 2):
            u[d, group * (Z // 2) + zz] = total[zz]
        for k in range(1, Z):
            pl.when(far[k] // (Z // 2) == group)(to_z[d, k].start)

    def got_tile(j):
        g_copy(j).wait_recv()
        g_store(1, j).start()
        acc_t[1] += input_part(we[j], g_got[j].astype(f32))

    for d in chunks:
        over_c(0, d, acc_t[0, d * wide : (d + 1) * wide])
    pl.loop(0, 2)(got_tile)
    for d in chunks:
        over_y(0, d)
    pl.loop(2, 5)(got_tile)
    for d in chunks:
        over_z(0, d)
    pl.loop(5, NT - 1)(got_tile)
    g_copy(NT - 1).wait_recv()
    g_store(1, NT - 1).start()
    last = g_got[NT - 1].astype(f32)
    for d in chunks:
        at = slice(d * wide, (d + 1) * wide)
        over_c(1, d, acc_t[1, at] + input_part(we[NT - 1, at], last))
    for d in chunks:
        over_y(1, d)
    for d in chunks:
        over_z(1, d)
    for d in chunks:
        terms = [u[d, z]]
        for k in range(1, Z):
            to_z[d, k].wait_recv()
            terms.append(rz[d, k])
        for layer in range(S):
            total = jnp.zeros_like(terms[0])
            for k in range(Z):
                total = total + jnp.where(near[k] // (Z // S) == layer, terms[k], 0.0)
            in_out[layer, :, d * wide : (d + 1) * wide] = total

    for copy in xz + ez + xy + xc + ey + ec + [sq_copy] + [*to_c.values(), *to_y.values(), *to_z.values()]:
        copy.wait_send()
    for j in range(NT):
        pre_copy(j).wait_send()
        dact_copy(j).wait_send()
        g_copy(j).wait_send()
        g_store(0, j).wait()
        g_store(1, j).wait()
    own_store.wait()


def encoder_kernel(own_ref, g_ref, in_ref, enc_hbm, bias_out, in_out, enc, sem):
    step = enc.shape[1]

    def store(i):
        return pltpu.make_async_copy(enc.at[i], enc_hbm.at[pl.ds(i * step, step)], sem.at[i])

    @pl.loop(0, enc.shape[0])
    def _(i):
        enc[i] = jnp.dot(
            own_ref[pl.ds(i * step, step)], g_ref[...], preferred_element_type=jnp.float32
        )
        store(i).start()

    half = g_ref.shape[0] // 2
    sums = [
        jnp.sum(g_ref[h * half : h * half + half].astype(jnp.float32), axis=0, keepdims=True)
        for h in range(2)
    ]
    bias_out[...] = sums[0] + sums[1]
    for layer in range(S):
        in_out[:, layer, :] = in_ref[layer]
    for i in range(enc.shape[0]):
        store(i).wait()


def local_kernel(inputs, w_enc, b_enc, masks, w_dec, errors, target_of):
    rows, _, width = inputs.shape
    tokens, block = masks.shape
    full = w_dec.shape[2]
    f32, bf16 = jnp.float32, jnp.bfloat16
    vmem = pltpu.VMEM
    dma = pltpu.SemaphoreType.DMA
    hbm = pl.BlockSpec(memory_space=pltpu.HBM)
    free, whole = pl.BlockSpec(memory_space=pl.ANY), pl.BlockSpec(memory_space=pltpu.VMEM)
    tiles = (NT, tokens // 2, TILE)
    wide = width // CHUNKS
    grad, own_t, grad_in = pl.pallas_call(
        kernel,
        out_shape=(
            jax.ShapeDtypeStruct((tokens, block), bf16),
            jax.ShapeDtypeStruct((width, tokens), bf16),
            jax.ShapeDtypeStruct((S, rows, width), f32),
        ),
        in_specs=[hbm] * 6 + [pl.BlockSpec(memory_space=pltpu.SMEM)],
        out_specs=(free, free, whole),
        scratch_shapes=[
            vmem((NT, width, TILE), bf16),
            vmem((NT, TILE, full), bf16),
            vmem(tiles, jnp.int32),
            vmem((1, block), f32),
            vmem((rows, S, width), bf16),
            vmem((S, rows, width), bf16),
            vmem((2, Z * 2, rows, width), bf16),
            vmem((2, Z * 2, rows, full), bf16),
            vmem((tokens, width), bf16),
            vmem((width, tokens), bf16),
            vmem((tokens, full), bf16),
            vmem((full, tokens), bf16),
            vmem(tiles, bf16), vmem(tiles, bf16), vmem(tiles, bf16), vmem(tiles, bf16),
            vmem((NT, 1, TILE), f32), vmem((NT, 1, TILE), f32),
            vmem(tiles, f32), vmem(tiles, f32),
            vmem(tiles, bf16), vmem(tiles, bf16),
            vmem((2, width, tokens // 2), f32),
            vmem((2, CHUNKS, 2, 2, Z // 2, rows, wide), f32),
            vmem((2, CHUNKS, 2, Z // 2, rows, wide), f32),
            vmem((2, CHUNKS, 2, Z // 2, rows, wide), bf16),
            vmem((2, CHUNKS, Z // 2, rows, wide), bf16),
            vmem((CHUNKS, Z, rows, wide), f32),
            vmem((CHUNKS, Z, rows, wide), f32),
            dma((3 * NT + 3,)),
        ]
        + [dma((Z,))] * 12
        + [dma((NT,))] * 4
        + [dma((1,))] * 2
        + [dma((NT,))] * 2
        + [dma((2, CHUNKS))] * 4
        + [dma((CHUNKS, Z))] * 2
        + [dma((2 * NT + 1,))],
        compiler_params=pltpu.CompilerParams(
            collective_id=0, has_side_effects=True, vmem_limit_bytes=62 * 1024 * 1024
        ),
    )(inputs, w_enc, b_enc[None, :], masks, w_dec, errors, target_of)
    grad_enc, bias, grad_in = pl.pallas_call(
        encoder_kernel,
        out_shape=(
            jax.ShapeDtypeStruct((width, block), f32),
            jax.ShapeDtypeStruct((1, block), f32),
            jax.ShapeDtypeStruct((rows, S, width), f32),
        ),
        in_specs=[whole] * 3,
        out_specs=(free, whole, whole),
        scratch_shapes=[vmem((6, width // 6, block), f32), dma((6,))],
        compiler_params=pltpu.CompilerParams(vmem_limit_bytes=62 * 1024 * 1024),
    )(own_t, grad, grad_in)
    return grad_enc, bias[0], grad_in


def solution(mesh):
    sizes = dict(mesh.shape)
    fits = sizes["lat"] == 4 * Z and sizes["tgt"] == 2
    return jax.shard_map(
        local_kernel if fits else local_any,
        mesh=mesh,
        in_specs=(
            P("lat", None, "tgt"),
            P("tgt", "lat"),
            P("lat"),
            P(None, "lat"),
            P("tgt", "lat", None),
            P("tgt", "lat", None),
            P(),
        ),
        out_specs=(P("tgt", "lat"), P("lat"), P("lat", None, "tgt")),
        check_vma=False,
    )
```

time: 52.8 us -> 50.6 us (0.958)
  the two profiles are of different devices: /device:TPU:0 before, /device:TPU:2 now
where the time goes in v4:
time: 50.6 us; the launch traced here: 50.4 us
  Pallas kernels  49.8 us (98%)
  between operations  0.64 us (1%)
    pallas_call x1, Pallas kernels, local_kernel(): pl.pallas_call(kernel, out_shape=(jax.ShapeDtypeStruct((tokens, block), b...  44 us
    pallas_call x1, Pallas kernels, local_kernel(): pl.pallas_call(encoder_kernel, out_shape=(jax.ShapeDtypeStruct((width, bl...  5.82 us

profile of v4, /device:TPU:2, one launch (start us, length us, event | category | flops | bytes accessed | tf_op | source)
XLA Modules:
  0.0 50.4 jit_solution(10831982352384921308)
XLA Ops:
  0.6 44.0 %shard_map.94 = (bf16[128,2048]{1,0:T(8,128)(2,1)}, bf16[1152,128]{1,0:T(8,128)(2,1)}, f32[2,8,1152]{2,1,0:T(8,128)}) custom-call(bf16[8,2,1152]{2,1,0:T(2,128)(2,1)} %x_hbm.1, bf16[1152,2048]{1,0:T(8,128)(2,1)} %we_hbm.1, f32[1,2048]{1,0:T(1,128)} %bitcast.2, s32[128,2048]{1,0:T(8,128)} %mask_hbm.1, bf16[1,2048,2304]{2,1,0:T(8,128)(2,1)} %wd_hbm.1, ...), custom_call_target="tpu_custom_call" | custom-call | tf_op jit(solution)/shard_map/pallas_call | solution.py:402
  44.6 5.8 %shard_map.95 = (f32[1152,2048]{1,0:T(8,128)}, f32[1,2048]{1,0:T(1,128)}, f32[8,2,1152]{2,1,0:T(2,128)}) custom-call(bf16[1152,128]{1,0:T(8,128)(2,1)} %get-tuple-element.9.own_ref, bf16[128,2048]{1,0:T(8,128)(2,1)} %get-tuple-element.10.g_ref, f32[2,8,1152]{2,1,0:T(8,128)} %get-tuple-element.11.in_ref), custom_call_target="tpu_custom_call" | custom-call | tf_op jit(solution)/shard_map/pallas_call | solution.py:448

commit v5 on v4

--- a/solution.py
+++ b/solution.py
@@ -166,16 +166,14 @@
     xy, xc = along_y(xs, xy_s, xy_r), along_c(xs, xc_s, xc_r)
     ey, ec = along_y(es, ey_s, ey_r), along_c(es, ec_s, ec_r)
 
-    def z_to_y(along_z, y_copies):
-        y_copies[0].start()
-        for k in range(1, Z):
+    def z_to_y(along_z, y_copies, k):
+        if k:
             along_z[k - 1].wait_recv()
-            y_copies[k].start()
-
-    def y_to_c(y_copies, c_copies):
-        for k in range(Z):
-            y_copies[k].wait_recv()
-            c_copies[k].start()
+        y_copies[k].start()
+
+    def y_to_c(y_copies, c_copies, k):
+        y_copies[k].wait_recv()
+        c_copies[k].start()
 
     def squares(j):
         wd_load(j).wait()
@@ -187,18 +185,19 @@
 
     flag = jnp.where(target_ref[t] >= source, 1.0, 0.0).astype(f32)
 
-    z_to_y(xz, xy)
+    for k in range(Z):
+        z_to_y(xz, xy, k)
     for copy in ez:
         copy.start()
     squares(0)
-    y_to_c(xy, xc)
+    for k in range(Z):
+        y_to_c(xy, xc, k)
     for j in range(NT):
         mask_load(j).start()
     b_load.start()
+    e_load.wait()
+    z_to_y(ez, ey, 0)
     squares(1)
-    e_load.wait()
-    z_to_y(ez, ey)
-    pl.loop(2, 4)(squares)
     for copy in xc:
         copy.wait_recv()
 
@@ -220,15 +219,14 @@
         pre_send[j] = part[half:].astype(jnp.bfloat16)
         pre_copy(j).start()
 
-    pl.loop(0, NT)(pre_tile)
-    y_to_c(ey, ec)
-    pl.loop(4, NT)(squares)
-    sq_copy = remote(sq_own, sq_got, sq_s.at[0], sq_r.at[0], x_peer)
-    sq_copy.start()
-    for at in range(0, xg.shape[1], 128):
-        own_t[at : at + 128] = xg[:, at : at + 128].astype(f32).T.astype(jnp.bfloat16)
-    own_store = pltpu.make_async_copy(own_t, own_out, out_sem.at[2 * NT])
-    own_store.start()
+    pl.loop(0, 2)(pre_tile)
+    for k in range(1, Z):
+        z_to_y(ez, ey, k)
+        pre_tile(k + 1)
+    pl.loop(Z + 1, NT)(pre_tile)
+    for k in range(Z):
+        squares(k + 2)
+        y_to_c(ey, ec, k)
     for copy in ec:
         copy.wait_recv()
     tokens_of(es, eg)
@@ -244,9 +242,13 @@
         dact_send[j] = part[half:].astype(jnp.bfloat16)
         dact_copy(j).start()
 
-    pl.loop(0, NT)(dact_tile)
-    b_load.wait()
-    sq_copy.wait_recv()
+    @pl.loop(0, 2)
+    def _(j):
+        dact_tile(j)
+        squares(j + NT - 2)
+
+    sq_copy = remote(sq_own, sq_got, sq_s.at[0], sq_r.at[0], x_peer)
+    sq_copy.start()
 
     def g_copy(j):
         return remote(g_own.at[j], g_got.at[j], g_s.at[j], g_r.at[j], x_peer)
@@ -277,7 +279,17 @@
         g_store(0, j).start()
         acc_t[0] += input_part(we[j], grad.astype(f32))
 
-    pl.loop(0, NT)(grad_tile)
+    lag = 4
+    pl.loop(2, lag)(dact_tile)
+    b_load.wait()
+    sq_copy.wait_recv()
+
+    @pl.loop(lag, NT)
+    def _(j):
+        dact_tile(j)
+        grad_tile(j - lag)
+
+    pl.loop(NT - lag, NT)(grad_tile)
 
     chunks = range(rs.shape[1])
     wide = rs.shape[-1]
@@ -327,6 +339,10 @@
     pl.loop(0, 2)(got_tile)
     for d in chunks:
         over_y(0, d)
+    for at in range(0, xg.shape[1], 128):
+        own_t[at : at + 128] = xg[:, at : at + 128].astype(f32).T.astype(jnp.bfloat16)
+    own_store = pltpu.make_async_copy(own_t, own_out, out_sem.at[2 * NT])
+    own_store.start()
     pl.loop(2, 5)(got_tile)
     for d in chunks:
         over_z(0, d)

time: 50.6 us -> 53.6 us (1.059)
  Pallas kernels: 49.8 us -> 52.8 us
    pallas_call x1, Pallas kernels: 44 us -> 47 us  [local_kernel(): pl.pallas_call(kernel, out_shape=(jax.ShapeDtypeStruct((tokens, block), b...]
where the time goes in v5:
time: 53.6 us; the launch traced here: 53.4 us
  Pallas kernels  52.8 us (99%)
  between operations  0.64 us (1%)
    pallas_call x1, Pallas kernels, local_kernel(): pl.pallas_call(kernel, out_shape=(jax.ShapeDtypeStruct((tokens, block), b...  47 us
    pallas_call x1, Pallas kernels, local_kernel(): pl.pallas_call(encoder_kernel, out_shape=(jax.ShapeDtypeStruct((width, bl...  5.81 us

profile of v5, /device:TPU:2, one launch (start us, length us, event | category | flops | bytes accessed | tf_op | source)
XLA Modules:
  0.0 53.4 jit_solution(1091787091863463386)
XLA Ops:
  0.6 47.0 %shard_map.94 = (bf16[128,2048]{1,0:T(8,128)(2,1)}, bf16[1152,128]{1,0:T(8,128)(2,1)}, f32[2,8,1152]{2,1,0:T(8,128)}) custom-call(bf16[8,2,1152]{2,1,0:T(2,128)(2,1)} %x_hbm.1, bf16[1152,2048]{1,0:T(8,128)(2,1)} %we_hbm.1, f32[1,2048]{1,0:T(1,128)} %bitcast.2, s32[128,2048]{1,0:T(8,128)} %mask_hbm.1, bf16[1,2048,2304]{2,1,0:T(8,128)(2,1)} %wd_hbm.1, ...), custom_call_target="tpu_custom_call" | custom-call | tf_op jit(solution)/shard_map/pallas_call | solution.py:418
  47.6 5.8 %shard_map.95 = (f32[1152,2048]{1,0:T(8,128)}, f32[1,2048]{1,0:T(1,128)}, f32[8,2,1152]{2,1,0:T(2,128)}) custom-call(bf16[1152,128]{1,0:T(8,128)(2,1)} %get-tuple-element.9.own_ref, bf16[128,2048]{1,0:T(8,128)(2,1)} %get-tuple-element.10.g_ref, f32[2,8,1152]{2,1,0:T(8,128)} %get-tuple-element.11.in_ref), custom_call_target="tpu_custom_call" | custom-call | tf_op jit(solution)/shard_map/pallas_call | solution.py:464

commit v6 on v5

--- a/solution.py
+++ b/solution.py
@@ -185,19 +185,21 @@
 
     flag = jnp.where(target_ref[t] >= source, 1.0, 0.0).astype(f32)
 
-    for k in range(Z):
-        z_to_y(xz, xy, k)
+    z_to_y(xz, xy, 0)
     for copy in ez:
         copy.start()
+    e_load.wait()
+    z_to_y(ez, ey, 0)
+    for k in range(1, Z):
+        z_to_y(xz, xy, k)
     squares(0)
     for k in range(Z):
         y_to_c(xy, xc, k)
     for j in range(NT):
         mask_load(j).start()
     b_load.start()
-    e_load.wait()
-    z_to_y(ez, ey, 0)
-    squares(1)
+    for k in range(1, Z):
+        z_to_y(ez, ey, k)
     for copy in xc:
         copy.wait_recv()
 
@@ -219,14 +221,13 @@
         pre_send[j] = part[half:].astype(jnp.bfloat16)
         pre_copy(j).start()
 
-    pl.loop(0, 2)(pre_tile)
-    for k in range(1, Z):
-        z_to_y(ez, ey, k)
-        pre_tile(k + 1)
-    pl.loop(Z + 1, NT)(pre_tile)
-    for k in range(Z):
-        squares(k + 2)
+    pl.loop(0, 4)(pre_tile)
+    for k in range(2):
         y_to_c(ey, ec, k)
+    pl.loop(4, NT)(pre_tile)
+    for k in range(2, Z):
+        y_to_c(ey, ec, k)
+    pl.loop(1, 4)(squares)
     for copy in ec:
         copy.wait_recv()
     tokens_of(es, eg)
@@ -242,10 +243,10 @@
         dact_send[j] = part[half:].astype(jnp.bfloat16)
         dact_copy(j).start()
 
-    @pl.loop(0, 2)
+    @pl.loop(0, 4)
     def _(j):
         dact_tile(j)
-        squares(j + NT - 2)
+        squares(j + 4)
 
     sq_copy = remote(sq_own, sq_got, sq_s.at[0], sq_r.at[0], x_peer)
     sq_copy.start()
@@ -280,7 +281,6 @@
         acc_t[0] += input_part(we[j], grad.astype(f32))
 
     lag = 4
-    pl.loop(2, lag)(dact_tile)
     b_load.wait()
     sq_copy.wait_recv()
 

time: 53.6 us -> 54.5 us (1.017)
  Pallas kernels: 52.8 us -> 53.7 us
    pallas_call x1, Pallas kernels: 47 us -> 47.9 us  [local_kernel(): pl.pallas_call(kernel, out_shape=(jax.ShapeDtypeStruct((tokens, block), b...]
where the time goes in v6:
time: 54.5 us; the launch traced here: 54.4 us
  Pallas kernels  53.7 us (99%)
  between operations  0.64 us (1%)
    pallas_call x1, Pallas kernels, local_kernel(): pl.pallas_call(kernel, out_shape=(jax.ShapeDtypeStruct((tokens, block), b...  47.9 us
    pallas_call x1, Pallas kernels, local_kernel(): pl.pallas_call(encoder_kernel, out_shape=(jax.ShapeDtypeStruct((width, bl...  5.81 us

profile of v6, /device:TPU:2, one launch (start us, length us, event | category | flops | bytes accessed | tf_op | source)
XLA Modules:
  0.0 54.4 jit_solution(1241402002998718479)
XLA Ops:
  0.6 47.9 %shard_map.94 = (bf16[128,2048]{1,0:T(8,128)(2,1)}, bf16[1152,128]{1,0:T(8,128)(2,1)}, f32[2,8,1152]{2,1,0:T(8,128)}) custom-call(bf16[8,2,1152]{2,1,0:T(2,128)(2,1)} %x_hbm.1, bf16[1152,2048]{1,0:T(8,128)(2,1)} %we_hbm.1, f32[1,2048]{1,0:T(1,128)} %bitcast.2, s32[128,2048]{1,0:T(8,128)} %mask_hbm.1, bf16[1,2048,2304]{2,1,0:T(8,128)(2,1)} %wd_hbm.1, ...), custom_call_target="tpu_custom_call" | custom-call | tf_op jit(solution)/shard_map/pallas_call | solution.py:418
  48.6 5.8 %shard_map.95 = (f32[1152,2048]{1,0:T(8,128)}, f32[1,2048]{1,0:T(1,128)}, f32[8,2,1152]{2,1,0:T(2,128)}) custom-call(bf16[1152,128]{1,0:T(8,128)(2,1)} %get-tuple-element.9.own_ref, bf16[128,2048]{1,0:T(8,128)(2,1)} %get-tuple-element.10.g_ref, f32[2,8,1152]{2,1,0:T(8,128)} %get-tuple-element.11.in_ref), custom_call_target="tpu_custom_call" | custom-call | tf_op jit(solution)/shard_map/pallas_call | solution.py:464
